TPU v7x, 1024 devices: a whole 4x8x16 slice. The times are simulated.
1024 devices in a mesh: grp: 32 (over x, y), peer: 32 (over z, core).
Axes of the slice: x: 4, y: 8, z: 16, core: 2. Of those that a mesh axis runs over, the one named last changes fastest.
Arguments:
- labels: bfloat16 [1048576, 256], P(('grp', 'peer')), may hold values from -6 to 6
- node_degree: int32 [1048576], P(('grp', 'peer')), may hold values from 1 to 64
- edge_degree: int32 [524288], P(('grp', 'peer')), may hold values from 1 to 64
- labeled_mask: int32 [1048576], P(('grp', 'peer')), may hold values 0 or 1
- seed_labels: int32 [1048576], P(('grp', 'peer')), may hold values from 0 to 255
- local_incidence: bfloat16 [1048576, 512], P(('grp', 'peer')), may hold values from -0.25 to 0.25
- tiles: bfloat16 [1024, 64, 32, 16], P(('grp', 'peer')), may hold values from -1.5 to 1.5
- out_block: int32 [1024, 64], P(('grp', 'peer')), may hold values from 0 to 31
- out_count: int32 [1024, 64], P(('grp', 'peer')), may hold values 0 or 1
- in_edge: int32 [1024, 64], P(('grp', 'peer')), may hold values from 0 to 31
Outputs:
- spread_labels: bfloat16 [1048576, 256], P(('grp', 'peer'))
All inputs are finite; a program needn't handle non-finite values. No bound on the sum of `labeled_mask` or of `out_count` on one device may be relied on, other than what follows from the above.
Results may differ from a plain program's by a relative error of at most 0.008.
Values may be sent and summed in bfloat16 or wider, within the bound.
A program may use at most 32 MiB of HBM per device.

v0:
```python
import jax
import jax.numpy as jnp
from jax import lax
from jax.sharding import PartitionSpec as P

ROUNDS = 2


eps = 1e-05


def local(
    labels,
    node_degree,
    edge_degree,
    labeled_mask,
    seed_labels,
    local_incidence,
    tiles,
    out_block,
    out_count,
    in_edge,
):
    n_peer = lax.axis_size("peer")
    row_count, classes = labels.shape
    edge_count = local_incidence.shape[1]
    slot_count = tiles.shape[1]
    block_rows = tiles.shape[2]
    tile_width = tiles.shape[3]
    n_blocks = row_count // block_rows
    e_blocks = edge_count // tile_width
    tile_set = tiles[0]
    live_slots = out_count[0].astype(jnp.float32)
    pick_rows = (out_block[0][:, None] == jnp.arange(n_blocks, dtype=jnp.int32)[None, :]).astype(
        jnp.float32
    ) * live_slots[:, None]
    pick_send = pick_rows.astype(jnp.bfloat16)
    pick_edge = (in_edge[0][:, None] == jnp.arange(e_blocks, dtype=jnp.int32)[None, :]).astype(
        jnp.float32
    )
    pick_agg = pick_edge.astype(jnp.bfloat16)
    node_scale = lax.rsqrt(node_degree.astype(jnp.float32))[:, None]
    edge_div = edge_degree.astype(jnp.float32)[:, None]
    labeled = (labeled_mask == 1)[:, None]
    seed_rows = jnp.sqrt(jnp.float32(classes)) * (
        seed_labels[:, None] == jnp.arange(classes, dtype=jnp.int32)[None, :]
    ).astype(jnp.float32)
    current = labels
    for round_index in range(ROUNDS):
        scaled = (current.astype(jnp.float32) * node_scale).astype(jnp.bfloat16)
        outgoing = jnp.dot(
            pick_send,
            scaled.reshape(n_blocks, block_rows * classes),
            preferred_element_type=jnp.float32,
        )
        outgoing = outgoing.astype(jnp.bfloat16).reshape(slot_count, block_rows, classes)
        local_edge = lax.dot_general(
            local_incidence, scaled, (((0,), (0,)), ((), ())), preferred_element_type=jnp.float32
        )
        label_peer, tile_peer = (
            lax.all_to_all(outgoing[:n_peer], "peer", split_axis=0, concat_axis=0, tiled=True),
            lax.all_to_all(tile_set[:n_peer], "peer", split_axis=0, concat_axis=0, tiled=True),
        )
        label_grp, tile_grp = (
            lax.all_to_all(outgoing[n_peer:], "grp", split_axis=0, concat_axis=0, tiled=True),
            lax.all_to_all(tile_set[n_peer:], "grp", split_axis=0, concat_axis=0, tiled=True),
        )
        arrived = jnp.concatenate([label_peer, label_grp], axis=0)
        tile_in = jnp.concatenate([tile_peer, tile_grp], axis=0)
        incoming = jnp.einsum("sbw,sbc->swc", tile_in, arrived, preferred_element_type=jnp.float32)
        remote_edge = jnp.dot(
            pick_edge.T,
            incoming.reshape(slot_count, tile_width * classes),
            precision=lax.Precision.HIGHEST,
            preferred_element_type=jnp.float32,
        )
        edge_total = local_edge + remote_edge.reshape(edge_count, classes)
        aggregate = (edge_total / edge_div).astype(jnp.bfloat16)
        chosen = jnp.dot(
            pick_agg,
            aggregate.reshape(e_blocks, tile_width * classes),
            preferred_element_type=jnp.float32,
        )
        chosen = chosen.astype(jnp.bfloat16).reshape(slot_count, tile_width, classes)
        local_node = jnp.dot(local_incidence, aggregate, preferred_element_type=jnp.float32)
        product = jnp.einsum("sbw,swc->sbc", tile_in, chosen, preferred_element_type=jnp.float32)
        back_peer = lax.all_to_all(
            product[:n_peer], "peer", split_axis=0, concat_axis=0, tiled=True
        )
        back_grp = lax.all_to_all(product[n_peer:], "grp", split_axis=0, concat_axis=0, tiled=True)
        returned = jnp.concatenate([back_peer, back_grp], axis=0)
        remote_node = jnp.dot(
            pick_rows.T,
            returned.reshape(slot_count, block_rows * classes),
            precision=lax.Precision.HIGHEST,
            preferred_element_type=jnp.float32,
        )
        node_total = local_node + remote_node.reshape(row_count, classes)
        mean_square = jnp.mean(node_total * node_total, axis=-1, keepdims=True)
        normed = node_total * lax.rsqrt(mean_square + eps)
        current = jnp.where(labeled, seed_rows, normed).astype(jnp.bfloat16)
    return current


def solution(mesh):
    placed = (
        P(("grp", "peer"), None),
        P(("grp", "peer")),
        P(("grp", "peer")),
        P(("grp", "peer")),
        P(("grp", "peer")),
        P(("grp", "peer"), None),
        P(("grp", "peer"), None, None, None),
        P(("grp", "peer"), None),
        P(("grp", "peer"), None),
        P(("grp", "peer"), None),
    )
    return jax.shard_map(
        local, mesh=mesh, in_specs=placed, out_specs=P(("grp", "peer"), None), check_vma=False
    )
```

profile of v0, /device:TPU:6, one launch (start us, length us, event | category | flops | bytes accessed | tf_op | source)
XLA Modules:
  0.0 379.1 jit_solution(11281898435641640502)
XLA Ops:
  0.0 1.2 fusion.50
  1.2 0.2 copy.28
  1.4 0.8 reshape.94
  2.1 16.8 %all-to-all-start.1 = ((bf16[32,2,256]{2,1,0:T(2,128)(2,1)}), bf16[32,2,256]{2,1,0:T(2,128)(2,1)S(1)}, u32[]{:S(2)}, u32[]{:S(2)}) async-start(bf16[32,2,256]{2,1,0:T(2,128)(2,1)} %reshape.94), calls=%async_computation.1 | async-start | bytes 65536 | tf_op jit(solution)/shard_map/all_to_all | solution.py:66
  18.9 0.7 convert_bitcast_fusion
  19.6 0.7 convert_rsqrt_fusion
  20.3 1.3 copy.15
  21.7 0.2 copy.18
  21.9 0.2 reshape.78
  22.1 0.2 copy.27
  22.3 0.5 convolution_convert_fusion.1
  22.8 0.8 reshape.92
  23.6 3.3 all-to-all-done.1
  26.9 12.7 %all-to-all-start = ((bf16[32,2,256]{2,1,0:T(2,128)(2,1)}), bf16[32,2,256]{2,1,0:T(2,128)(2,1)S(1)}, u32[]{:S(2)}, u32[]{:S(2)}) async-start(bf16[32,2,256]{2,1,0:T(2,128)(2,1)} %reshape.92), calls=%async_computation | async-start | bytes 65536 | tf_op jit(solution)/shard_map/all_to_all | solution.py:62
  39.7 0.9 copy.30
  40.6 12.0 %all-to-all-done = bf16[32,2,256]{2,1,0:T(2,128)(2,1)S(1)} async-done(((bf16[32,2,256]{2,1,0:T(2,128)(2,1)}), bf16[32,2,256]{2,1,0:T(2,128)(2,1)S(1)}, u32[]{:S(2)}, u32[]{:S(2)}) %all-to-all-start) | async-done | bytes 32800 | tf_op jit(solution)/shard_map/all_to_all | solution.py:62
  52.6 6.4 %all-to-all-start.3 = ((bf16[32,32,256]{2,1,0:T(8,128)(2,1)}), bf16[32,32,256]{2,1,0:T(8,128)(2,1)S(1)}, u32[]{:S(2)}, u32[]{:S(2)}) async-start(bf16[32,32,256]{2,1,0:T(8,128)(2,1)} %bitcast.12), calls=%async_computation.3 | async-start | bytes 1048576 | tf_op jit(solution)/shard_map/all_to_all | solution.py:65
  59.0 0.9 copy.29
  59.9 13.8 %all-to-all-done.3 = bf16[32,32,256]{2,1,0:T(8,128)(2,1)S(1)} async-done(((bf16[32,32,256]{2,1,0:T(8,128)(2,1)}), bf16[32,32,256]{2,1,0:T(8,128)(2,1)S(1)}, u32[]{:S(2)}, u32[]{:S(2)}) %all-to-all-start.3) | async-done | bytes 524320 | tf_op jit(solution)/shard_map/all_to_all | solution.py:65
  73.7 3.9 %all-to-all-start.2 = ((bf16[32,32,256]{2,1,0:T(8,128)(2,1)}), bf16[32,32,256]{2,1,0:T(8,128)(2,1)S(1)}, u32[]{:S(2)}, u32[]{:S(2)}) async-start(bf16[32,32,256]{2,1,0:T(8,128)(2,1)} %bitcast.10), calls=%async_computation.2 | async-start | bytes 1048576 | tf_op jit(solution)/shard_map/all_to_all | solution.py:61
  77.9 33.7 %all-to-all-done.2 = bf16[32,32,256]{2,1,0:T(8,128)(2,1)S(1)} async-done(((bf16[32,32,256]{2,1,0:T(8,128)(2,1)}), bf16[32,32,256]{2,1,0:T(8,128)(2,1)S(1)}, u32[]{:S(2)}, u32[]{:S(2)}) %all-to-all-start.2) | async-done | bytes 524320 | tf_op jit(solution)/shard_map/all_to_all | solution.py:61
  111.6 0.3 fusion.10
  111.9 0.6 copy.31
  112.5 0.5 fusion.23
  113.2 0.2 copy.19
  113.4 1.1 fusion.6
  114.5 1.1 copy.20
  115.7 0.3 convolution_convert_fusion.3
  116.2 0.5 fusion.51
  116.7 1.2 fusion.47
  117.8 33.6 %all_to_all.52 = f32[32,32,256]{2,1,0:T(8,128)S(1)} all-to-all(f32[32,32,256]{2,1,0:T(8,128)S(1)} %get-tuple-element.8), channel_id=1, replica_groups=mesh['grp'=32,'peer'=32] {'grp'}, dimensions={0} | all-to-all | bytes 2097152 | tf_op jit(solution)/shard_map/all_to_all | solution.py:90
  151.4 4.1 %all-to-all-start.4 = ((f32[32,32,256]{2,1,0:T(8,128)}), f32[32,32,256]{2,1,0:T(8,128)S(1)}, u32[]{:S(2)}, u32[]{:S(2)}) async-start(f32[32,32,256]{2,1,0:T(8,128)} %get-tuple-element.7), calls=%async_computation.4 | async-start | bytes 2097152 | tf_op jit(solution)/shard_map/all_to_all | solution.py:87
  155.6 56.3 %all-to-all-done.4 = f32[32,32,256]{2,1,0:T(8,128)S(1)} async-done(((f32[32,32,256]{2,1,0:T(8,128)}), f32[32,32,256]{2,1,0:T(8,128)S(1)}, u32[]{:S(2)}, u32[]{:S(2)}) %all-to-all-start.4) | async-done | bytes 1048608 | tf_op jit(solution)/shard_map/all_to_all | solution.py:87
  211.9 0.2 pad_maximum_fusion
  212.1 1.2 copy.33
  213.3 1.2 fusion.20
  214.5 0.2 reshape.84
  214.7 0.3 copy.21
  215.0 1.4 multiply_reduce_fusion.1
  216.5 0.2 multiply_convert_fusion
  216.7 0.2 copy.22
  216.9 0.2 reshape.85
  217.2 0.5 convolution_convert_fusion
  217.7 0.9 copy.35
  218.7 7.3 %all-to-all-start.7 = ((bf16[32,32,256]{2,1,0:T(8,128)(2,1)}), bf16[32,32,256]{2,1,0:T(8,128)(2,1)S(1)}, u32[]{:S(2)}, u32[]{:S(2)}) async-start(bf16[32,32,256]{2,1,0:T(8,128)(2,1)} %bitcast.22), calls=%async_computation.7 | async-start | bytes 1048576 | tf_op jit(solution)/shard_map/all_to_all | solution.py:65
  226.0 14.6 %all-to-all-done.7 = bf16[32,32,256]{2,1,0:T(8,128)(2,1)S(1)} async-done(((bf16[32,32,256]{2,1,0:T(8,128)(2,1)}), bf16[32,32,256]{2,1,0:T(8,128)(2,1)S(1)}, u32[]{:S(2)}, u32[]{:S(2)}) %all-to-all-start.7) | async-done | bytes 524320 | tf_op jit(solution)/shard_map/all_to_all | solution.py:65
  240.6 37.0 %all_to_all.53 = bf16[32,32,256]{2,1,0:T(8,128)(2,1)S(1)} all-to-all(bf16[32,32,256]{2,1,0:T(8,128)(2,1)S(1)} %bitcast.90), channel_id=1, replica_groups=mesh['grp'=32,'peer'=32] {'peer'}, dimensions={0} | all-to-all | bytes 1048576 | tf_op jit(solution)/shard_map/all_to_all | solution.py:61
  277.6 0.3 fusion.14
  277.9 0.6 copy.36
  278.5 0.5 fusion.22
  279.1 0.2 copy.23
  279.3 0.4 fusion.7
  280.1 0.3 convolution_convert_fusion.2
  280.5 0.5 fusion.52
  281.0 0.2 fusion.46
  281.2 33.6 %all_to_all.54 = f32[32,32,256]{2,1,0:T(8,128)S(1)} all-to-all(f32[32,32,256]{2,1,0:T(8,128)S(1)} %get-tuple-element.6), channel_id=1, replica_groups=mesh['grp'=32,'peer'=32] {'grp'}, dimensions={0} | all-to-all | bytes 2097152 | tf_op jit(solution)/shard_map/all_to_all | solution.py:90
  314.8 59.5 %all_to_all.55 = f32[32,32,256]{2,1,0:T(8,128)S(1)} all-to-all(f32[32,32,256]{2,1,0:T(8,128)S(1)} %get-tuple-element.5), channel_id=1, replica_groups=mesh['grp'=32,'peer'=32] {'peer'}, dimensions={0} | all-to-all | bytes 2097152 | tf_op jit(solution)/shard_map/all_to_all | solution.py:87
  374.3 0.2 pad_maximum_fusion.1
  374.5 1.2 copy.38
  375.7 1.2 fusion.18
  377.1 0.3 copy.25
  377.4 0.5 multiply_reduce_fusion
  377.9 0.2 fusion.9
  378.1 1.0 copy.26
  (34 shorter events, 1.6 us)
Async XLA Ops:
  0.0 113.4 %copy-start = (bf16[1024,512]{1,0:T(8,128)(2,1)S(1)}, bf16[1024,512]{1,0:T(8,128)(2,1)}, u32[]{:S(2)}) copy-start(bf16[1024,512]{1,0:T(8,128)(2,1)} %param.15) | copy-start | bytes 3145732
  2.1 24.7 %all-to-all-start.1 = ((bf16[32,2,256]{2,1,0:T(2,128)(2,1)}), bf16[32,2,256]{2,1,0:T(2,128)(2,1)S(1)}, u32[]{:S(2)}, u32[]{:S(2)}) async-start(bf16[32,2,256]{2,1,0:T(2,128)(2,1)} %reshape.94), calls=%async_computation.1 | async-start | bytes 65536 | tf_op jit(solution)/shard_map/all_to_all | solution.py:66
  20.3 2.0 copy-start.2
  26.9 25.7 %all-to-all-start = ((bf16[32,2,256]{2,1,0:T(2,128)(2,1)}), bf16[32,2,256]{2,1,0:T(2,128)(2,1)S(1)}, u32[]{:S(2)}, u32[]{:S(2)}) async-start(bf16[32,2,256]{2,1,0:T(2,128)(2,1)} %reshape.92), calls=%async_computation | async-start | bytes 65536 | tf_op jit(solution)/shard_map/all_to_all | solution.py:62
  39.7 37.9 %copy-start.5 = (s32[512]{0:T(512)S(1)}, s32[512]{0:T(512)}, u32[]{:S(2)}) copy-start(s32[512]{0:T(512)} %param.12) | copy-start | bytes 6148
  52.6 21.1 %all-to-all-start.3 = ((bf16[32,32,256]{2,1,0:T(8,128)(2,1)}), bf16[32,32,256]{2,1,0:T(8,128)(2,1)S(1)}, u32[]{:S(2)}, u32[]{:S(2)}) async-start(bf16[32,32,256]{2,1,0:T(8,128)(2,1)} %bitcast.12), calls=%async_computation.3 | async-start | bytes 1048576 | tf_op jit(solution)/shard_map/all_to_all | solution.py:65
  73.7 37.9 %all-to-all-start.2 = ((bf16[32,32,256]{2,1,0:T(8,128)(2,1)}), bf16[32,32,256]{2,1,0:T(8,128)(2,1)S(1)}, u32[]{:S(2)}, u32[]{:S(2)}) async-start(bf16[32,32,256]{2,1,0:T(8,128)(2,1)} %bitcast.10), calls=%async_computation.2 | async-start | bytes 1048576 | tf_op jit(solution)/shard_map/all_to_all | solution.py:61
  77.9 34.6 %copy-start.3 = (s32[1,64]{1,0:T(1,128)S(1)}, s32[1,64]{1,0:T(1,128)}, u32[]{:S(2)}) copy-start(s32[1,64]{1,0:T(1,128)} %param.19) | copy-start | bytes 772
  117.8 37.7 %copy-start.4 = (s32[1024]{0:T(1024)S(1)}, s32[1024]{0:T(1024)}, u32[]{:S(2)}) copy-start(s32[1024]{0:T(1024)} %param.13) | copy-start | bytes 12292
  151.4 60.4 %all-to-all-start.4 = ((f32[32,32,256]{2,1,0:T(8,128)}), f32[32,32,256]{2,1,0:T(8,128)S(1)}, u32[]{:S(2)}, u32[]{:S(2)}) async-start(f32[32,32,256]{2,1,0:T(8,128)} %get-tuple-element.7), calls=%async_computation.4 | async-start | bytes 2097152 | tf_op jit(solution)/shard_map/all_to_all | solution.py:87
  215.0 1.5 copy-start.1
  218.7 21.9 %all-to-all-start.7 = ((bf16[32,32,256]{2,1,0:T(8,128)(2,1)}), bf16[32,32,256]{2,1,0:T(8,128)(2,1)S(1)}, u32[]{:S(2)}, u32[]{:S(2)}) async-start(bf16[32,32,256]{2,1,0:T(8,128)(2,1)} %bitcast.22), calls=%async_computation.7 | async-start | bytes 1048576 | tf_op jit(solution)/shard_map/all_to_all | solution.py:65
where the time goes:
time: 382 us; the launch traced here: 379 us
  blocking collectives  164 us (43%)
  waiting for transfers between devices  134 us (35%)
  starting transfers between devices  51.2 us (13%)
  local copies, waits for them, and re-layouts  17.7 us (5%)
  matrix products  10.2 us (3%)
    all_to_all x2, blocking collectives, local(): lax.all_to_all(product[n_peer:], 'grp', split_axis=0, concat_axis=0, tile...  67.1 us
    all_to_all x1, blocking collectives, local(): lax.all_to_all(product[:n_peer], 'peer', split_axis=0, concat_axis=0, til...  59.5 us
    all_to_all x1, waiting for transfers between devices, local(): lax.all_to_all(product[:n_peer], 'peer', split_axis=0, concat_axis=0, til...  56.3 us
    all_to_all x1, blocking collectives, local(): lax.all_to_all(outgoing[:n_peer], 'peer', split_axis=0, concat_axis=0, ti...  37 us
    all_to_all x1, waiting for transfers between devices, local(): lax.all_to_all(outgoing[:n_peer], 'peer', split_axis=0, concat_axis=0, ti...  33.7 us
    all_to_all x2, waiting for transfers between devices, local(): lax.all_to_all(outgoing[n_peer:], 'grp', split_axis=0, concat_axis=0, til...  28.3 us
    all_to_all x1, starting transfers between devices, local(): lax.all_to_all(tile_set[n_peer:], 'grp', split_axis=0, concat_axis=0, til...  16.8 us
    all_to_all x2, starting transfers between devices, local(): lax.all_to_all(outgoing[n_peer:], 'grp', split_axis=0, concat_axis=0, til...  13.7 us
  transfers between devices with their start and end apart: 6, of which 6 were waited for; matrix products, arithmetic and copies ran while one was open for 2% of the time, Pallas kernels for 0%

commit v1 on v0

v1 whole, which is shorter than its diff:
```python
import functools

import jax
import jax.numpy as jnp
from jax import lax
from jax.experimental import pallas as pl
from jax.experimental.pallas import tpu as pltpu
from jax.sharding import PartitionSpec as P

ROUNDS = 2
PARTS = 2
CHUNK = 16
LANES = 128
EPS = 1e-05
MESH = pl.DeviceIdType.MESH
F32 = jnp.float32
BF16 = jnp.bfloat16


def iota(shape, dim):
    return lax.broadcasted_iota(jnp.int32, shape, dim)


def dot(a, b):
    return jnp.dot(a, b, preferred_element_type=F32)


def dot_t(a, b):
    return lax.dot_general(a, b, (((1,), (1,)), ((), ())), preferred_element_type=F32)


def tiled(a, count):
    return a if count == 1 else jnp.concatenate([a] * count, axis=1)


def loop(count, body):
    def step(i, carry):
        body(i)
        return carry

    lax.fori_loop(0, count, step, 0)


def rows_of(i, count):
    return pl.ds(pl.multiple_of(i * count, count), count)


def kernel(
    sizes,
    labels_hbm,
    tiles_hbm,
    inc_hbm,
    node_hbm,
    edge_hbm,
    mask_hbm,
    seed_hbm,
    block_hbm,
    count_hbm,
    in_hbm,
    out_ref,
    labels,
    tiles,
    inc,
    node_ref,
    edge_ref,
    mask_ref,
    seed_ref,
    block_ref,
    count_ref,
    in_ref,
    out_buf,
    inc_t,
    spread,
    spread_t,
    choose,
    choose_t,
    tile_col,
    block_col,
    scale_col,
    seed_col,
    div_col,
    scaled,
    agg,
    edge_sum,
    node_sum,
    fsend,
    frecv,
    bsend,
    brecv,
    in_sem,
    out_sem,
    ready,
    fsend_sem,
    frecv_sem,
    bsend_sem,
    brecv_sem,
):
    n, slots, block, width, rows, edges, classes, chunk = sizes
    cols = classes // PARTS
    n_chunks = slots // chunk
    crows = chunk * width
    flat = slots * width
    fold = LANES // block
    g, p = lax.axis_index("grp"), lax.axis_index("peer")

    with jax.named_scope("greet"):
        moves = (
            (node_hbm, node_ref),
            (labels_hbm, labels),
            (tiles_hbm, tiles),
            (block_hbm, block_ref),
            (count_hbm, count_ref),
            (in_hbm, in_ref),
            (edge_hbm, edge_ref),
            (mask_hbm, mask_ref),
            (seed_hbm, seed_ref),
            (inc_hbm, inc),
        )
        loads = [pltpu.make_async_copy(src, dst, in_sem.at[k]) for k, (src, dst) in enumerate(moves)]
        for load in loads:
            load.start()

        barrier = pltpu.get_barrier_semaphore()

        def greet(j):
            @pl.when(j > p)
            def _():
                pl.semaphore_signal(barrier, inc=1, device_id=(g, j), device_id_type=MESH)

            @pl.when(j > g)
            def _():
                pl.semaphore_signal(barrier, inc=1, device_id=(j, p), device_id_type=MESH)

        loop(n, greet)

        @pl.when(p + g > 0)
        def _():
            pl.semaphore_wait(barrier, p + g)

        def answer(j):
            @pl.when(j < p)
            def _():
                pl.semaphore_signal(ready.at[p], inc=1, device_id=(g, j), device_id_type=MESH)

            @pl.when(j < g)
            def _():
                pl.semaphore_signal(ready.at[n + g], inc=1, device_id=(j, p), device_id_type=MESH)

        loop(n, answer)

    def column(ref):
        k, lanes = ref.shape
        pick = (iota((k, k * LANES), 1) // LANES == iota((k, k * LANES), 0)).astype(BF16)
        wide = lax.dot_general(ref[...].astype(F32).astype(BF16), pick, (((0,), (0,)), ((), ())), preferred_element_type=F32)
        return [wide[:, i * LANES : (i + 1) * LANES] for i in range(k)]

    with jax.named_scope("scale"):
        loads[0].wait()
        for i, part in enumerate(column(node_ref)):
            scale_col[i * LANES : (i + 1) * LANES, :] = lax.rsqrt(part)
        loads[1].wait()

        def scale_rows(i):
            at = rows_of(i, LANES)
            scaled[at, :] = (labels[at, :].astype(F32) * tiled(scale_col[at, :], classes // LANES)).astype(BF16)

        loop(rows // LANES, scale_rows)

    def pick_rows(i, value):
        slot = i * (LANES // width) + iota((LANES, slots), 0) // width
        return jnp.where(slot == iota((LANES, slots), 1), value, 0.0).astype(BF16)

    def slot_col(i, ref):
        return dot_t(pick_rows(i, 1.0), jnp.broadcast_to(ref[...].astype(F32), (LANES, slots)).astype(BF16))

    with jax.named_scope("tiles"):
        for load in loads[2:6]:
            load.wait()
        gather = (iota((block * width, LANES), 0) // width == iota((block * width, LANES), 1) % block).astype(BF16)

        def first_product(i):
            at = rows_of(i, LANES)
            wide = dot_t(pick_rows(i, count_ref[...].astype(F32)), tiles[...])
            same = iota((LANES, block * width), 0) % width == iota((LANES, block * width), 1) % width
            weight = dot(jnp.where(same, wide, 0.0).astype(BF16), gather)
            place = slot_col(i, block_ref)
            tile_col[at, :] = weight
            block_col[at, :] = place
            lane_block = (iota((LANES, LANES), 1) // block).astype(F32)
            parts = []
            for k in range(rows // LANES):
                piece = jnp.where(place == lane_block + float(k * fold), weight, 0.0).astype(BF16)
                spread_t[at, k * LANES : (k + 1) * LANES] = piece
                parts.append(piece)
            product = dot(jnp.concatenate(parts, axis=1), scaled[...]).astype(BF16)
            for h in range(PARTS):
                fsend[0, h, at, :] = product[:, h * cols : (h + 1) * cols]

        loop(flat // LANES, first_product)

    def copy_to(r, h, kind, other, src, dst, send_sem, recv_sem):
        me = g if kind else p
        pltpu.make_async_remote_copy(
            src_ref=src.at[r, h, rows_of(kind * n + other, width)],
            dst_ref=dst.at[r, h, rows_of(kind * n + me, width)],
            send_sem=send_sem.at[r, h],
            recv_sem=recv_sem.at[r, h, (kind * n + me) // chunk],
            device_id=(other, p) if kind else (g, other),
            device_id_type=MESH,
        ).start()

    def around(j, me):
        half = (j + 1) // 2
        return (me + n // 2 + half * (1 - 2 * (j % 2))) % n

    def send_all(r, h, *way):
        def one(j):
            copy_to(r, h, 0, around(j, p), *way)
            copy_to(r, h, 1, around(j, g), *way)

        loop(n - 1, one)

    def keep(r, h, src, dst, send_sem, recv_sem):
        for slot in (p, n + g):
            at = rows_of(slot, width)
            pltpu.make_async_copy(src.at[r, h, at], dst.at[r, h, at], recv_sem.at[r, h, slot // chunk]).start()

    def arrive(r, h, c, dst, recv_sem):
        part = dst.at[r, h, pl.ds(c * crows, crows)]
        pltpu.make_async_copy(part, part, recv_sem.at[r, h, c]).wait()

    out_way = (fsend, frecv, fsend_sem, frecv_sem)
    back_way = (bsend, brecv, bsend_sem, brecv_sem)

    with jax.named_scope("first_send"):

        def early(j):
            @pl.when(j < p)
            def _():
                copy_to(0, 0, 0, jnp.where(j % 2 == 0, j // 2, p - 1 - j // 2), *out_way)

            other = jnp.where(j < g, j, j + 1)

            @pl.when(j >= g)
            def _():
                pl.semaphore_wait(ready.at[n + other], 1)

            copy_to(0, 0, 1, other, *out_way)

        loop(n - 1, early)

        def late(j):
            @pl.when(j >= p)
            def _():
                pl.semaphore_wait(ready.at[j + 1], 1)
                copy_to(0, 0, 0, j + 1, *out_way)

        loop(n - 1, late)
        keep(0, 0, *out_way)
        for h in range(1, PARTS):
            send_all(0, h, *out_way)
            keep(0, h, *out_way)

    for r in range(ROUNDS):
        if r > 0:
            with jax.named_scope("out_send"):

                def product_rows(i):
                    at = rows_of(i, crows)
                    product = dot(spread_t[at, :], scaled[...]).astype(BF16)
                    for h in range(PARTS):
                        fsend[r, h, at, :] = product[:, h * cols : (h + 1) * cols]

                loop(n_chunks, product_rows)
                for h in range(PARTS):
                    send_all(r, h, *out_way)
                    keep(r, h, *out_way)
        else:
            with jax.named_scope("build"):
                for load in loads[6:]:
                    load.wait()

                for i, part in enumerate(column(edge_ref)):
                    div_col[i * LANES : (i + 1) * LANES, :] = part
                known, class_of = column(mask_ref), column(seed_ref)
                for i in range(rows // LANES):
                    seed_col[i * LANES : (i + 1) * LANES, :] = jnp.where(known[i] == 1.0, class_of[i], -1.0)

                for i in range(rows // LANES):
                    at = slice(i * LANES, (i + 1) * LANES)
                    inc_t[:, at] = inc[at, :].astype(F32).T.astype(BF16)

                for i in range(flat // LANES):
                    at = slice(i * LANES, (i + 1) * LANES)
                    row = (iota((LANES, LANES), 0) % width).astype(F32)
                    target = slot_col(i, in_ref) * float(width) + row
                    target_t = target.T
                    for k in range(edges // LANES):
                        e = slice(k * LANES, (k + 1) * LANES)
                        lane = (iota((LANES, LANES), 1) + k * LANES).astype(F32)
                        choose_t[at, e] = jnp.where(target == lane, 1.0, 0.0).astype(BF16)
                        down = (iota((LANES, LANES), 0) + k * LANES).astype(F32)
                        choose[e, at] = jnp.where(target_t == down, 1.0, 0.0).astype(BF16)
                    weight, place = tile_col[at, :].T, block_col[at, :].T
                    down_block = (iota((LANES, LANES), 0) // block).astype(F32)
                    for k in range(rows // LANES):
                        b = slice(k * LANES, (k + 1) * LANES)
                        spread[b, at] = jnp.where(place == down_block + float(k * fold), weight, 0.0).astype(BF16)

        with jax.named_scope("local_edge"):

            def local_edge(i):
                at = rows_of(i, 256)
                edge_sum[at, :] = dot(inc_t[at, :], scaled[...])

            loop(edges // 256, local_edge)

        for h in range(PARTS):
            part = slice(h * cols, (h + 1) * cols)
            with jax.named_scope("edge_wait"):
                for c in range(n_chunks):
                    arrive(r, h, c, frecv, frecv_sem)
            with jax.named_scope("edge"):

                def remote_edge(i):
                    at = rows_of(i, 256)
                    total = edge_sum[at, part] + dot(choose[at, :], frecv[r, h])
                    agg[at, part] = (total / tiled(div_col[at, :], cols // LANES)).astype(BF16)

                loop(edges // 256, remote_edge)
            with jax.named_scope("back_send"):

                def chosen(i):
                    at = rows_of(i, crows)
                    bsend[r, h, at, :] = dot(choose_t[at, :], agg[:, part]).astype(BF16)

                loop(n_chunks, chosen)
                send_all(r, h, *back_way)
                keep(r, h, *back_way)
            with jax.named_scope("local_node"):

                def local_node(i):
                    at = rows_of(i, 256)
                    node_sum[at, part] = dot(inc[at, :], agg[:, part])

                loop(rows // 256, local_node)

        for h in range(PARTS):
            part = slice(h * cols, (h + 1) * cols)
            with jax.named_scope("node_wait"):
                for c in range(n_chunks):
                    arrive(r, h, c, brecv, brecv_sem)
            if h == PARTS - 1:
                break
            with jax.named_scope("node"):

                def remote_node(i):
                    at = rows_of(i, 256)
                    node_sum[at, part] = node_sum[at, part] + dot(spread[at, :], brecv[r, h])

                loop(rows // 256, remote_node)

        with jax.named_scope("finish"):

            def finish(i):
                at = rows_of(i, LANES)
                last = dot(spread[at, :], brecv[r, PARTS - 1])
                total = node_sum[at, :]
                if PARTS > 1:
                    total = jnp.concatenate([total[:, : classes - cols], total[:, classes - cols :] + last], axis=1)
                else:
                    total = total + last
                mean_square = jnp.sum(total * total, axis=-1, keepdims=True) * (1.0 / classes)
                normed = total * lax.rsqrt(mean_square + EPS)
                known = tiled(seed_col[at, :], classes // LANES)
                seeds = jnp.where(iota((LANES, classes), 1).astype(F32) == known, float(classes) ** 0.5, 0.0)
                current = jnp.where(known >= 0.0, seeds, normed).astype(BF16)
                if r < ROUNDS - 1:
                    scaled[at, :] = (current.astype(F32) * tiled(scale_col[at, :], classes // LANES)).astype(BF16)
                else:
                    out_buf[at, :] = current

            loop(rows // LANES, finish)

    with jax.named_scope("store"):
        store = pltpu.make_async_copy(out_buf, out_ref, out_sem)
        store.start()
        for r in range(ROUNDS):
            for h in range(PARTS):
                for buf, sem in ((fsend, fsend_sem), (bsend, bsend_sem)):
                    sent = buf.at[r, h, pl.ds(0, (slots - 2) * width)]
                    pltpu.make_async_copy(sent, sent, sem.at[r, h]).wait()
        store.wait()


def local(labels, node_degree, edge_degree, labeled_mask, seed_labels, local_incidence, tiles, out_block, out_count, in_edge):
    n = lax.axis_size("peer")
    rows, classes = labels.shape
    edges = local_incidence.shape[1]
    _, slots, block, width = tiles.shape
    chunk = min(CHUNK, n)
    flat = slots * width
    sizes = (n, slots, block, width, rows, edges, classes, chunk)
    travel = (ROUNDS, PARTS, flat, classes // PARTS)
    hbm = pl.BlockSpec(memory_space=pltpu.HBM)
    dma = pltpu.SemaphoreType.DMA
    args = (
        labels,
        tiles[0].transpose(1, 2, 0).reshape(block * width, slots),
        local_incidence,
        node_degree.reshape(rows // LANES, LANES),
        edge_degree.reshape(edges // LANES, LANES),
        labeled_mask.reshape(rows // LANES, LANES),
        seed_labels.reshape(rows // LANES, LANES),
        out_block,
        out_count,
        in_edge,
    )
    return pl.pallas_call(
        functools.partial(kernel, sizes),
        out_shape=jax.ShapeDtypeStruct((rows, classes), BF16),
        in_specs=[hbm] * len(args),
        out_specs=pl.BlockSpec(memory_space=pl.ANY),
        scratch_shapes=[pltpu.VMEM(a.shape, a.dtype) for a in args]
        + [
            pltpu.VMEM((rows, classes), BF16),
            pltpu.VMEM((edges, rows), BF16),
            pltpu.VMEM((rows, flat), BF16),
            pltpu.VMEM((flat, rows), BF16),
            pltpu.VMEM((edges, flat), BF16),
            pltpu.VMEM((flat, edges), BF16),
            pltpu.VMEM((flat, LANES), F32),
            pltpu.VMEM((flat, LANES), F32),
            pltpu.VMEM((rows, LANES), F32),
            pltpu.VMEM((rows, LANES), F32),
            pltpu.VMEM((edges, LANES), F32),
            pltpu.VMEM((rows, classes), BF16),
            pltpu.VMEM((edges, classes), BF16),
            pltpu.VMEM((edges, classes), F32),
            pltpu.VMEM((rows, classes), F32),
            pltpu.VMEM(travel, BF16),
            pltpu.VMEM(travel, BF16),
            pltpu.VMEM(travel, BF16),
            pltpu.VMEM(travel, BF16),
            dma((len(args),)),
            dma,
            pltpu.SemaphoreType.REGULAR((slots,)),
            dma((ROUNDS, PARTS)),
            dma((ROUNDS, PARTS, slots // chunk)),
            dma((ROUNDS, PARTS)),
            dma((ROUNDS, PARTS, slots // chunk)),
        ],
        compiler_params=pltpu.CompilerParams(collective_id=0, has_side_effects=True, vmem_limit_bytes=60 << 20),
    )(*args)


def solution(mesh):
    split = ("grp", "peer")
    specs = (
        P(split, None),
        P(split),
        P(split),
        P(split),
        P(split),
        P(split, None),
        P(split, None, None, None),
        P(split, None),
        P(split, None),
        P(split, None),
    )
    return jax.shard_map(local, mesh=mesh, in_specs=specs, out_specs=P(split, None), check_vma=False)
```

time: 382 us -> 92.3 us (0.24)
  blocking collectives: 164 us -> 0 us
  waiting for transfers between devices: 134 us -> 0 us
  Pallas kernels: 0 us -> 90.2 us
  starting transfers between devices: 51.2 us -> 0 us
  local copies, waits for them, and re-layouts: 17.7 us -> 1.87 us
  matrix products: 10.2 us -> 0 us
    all_to_all x4 -> x0, blocking collectives: 164 us -> none  [the longest x2 67.1 us: local(): lax.all_to_all(product[n_peer:], 'grp', split_axis=0, concat_axis=0, tile...]
    all_to_all x6 -> x0, waiting for transfers between devices: 134 us -> none  [the longest x1 56.3 us: local(): lax.all_to_all(product[:n_peer], 'peer', split_axis=0, concat_axis=0, til...]
    pallas_call x0 -> x1, Pallas kernels: none -> 90.2 us  [local(): pl.pallas_call(functools.partial(kernel, sizes), out_shape=jax.ShapeDtype...]
    all_to_all x6 -> x0, starting transfers between devices: 51.2 us -> none  [the longest x1 16.8 us: local(): lax.all_to_all(tile_set[n_peer:], 'grp', split_axis=0, concat_axis=0, til...]
    dot_general x16 -> x0, matrix products: 10.2 us -> none  [the longest x2 2.4 us: local(): jnp.dot(pick_rows.T, returned.reshape(slot_count, block_rows * classes),...]
    unnamed x32 -> x1, local copies, waits for them, and re-layouts: 10.2 us -> 1.87 us
  transfers between devices with their start and end apart: 6 -> 0, of which waited for: 6 -> 0; matrix products, arithmetic and copies ran while one was open for 2% -> 0% of each run, Pallas kernels for 0% -> 0%
where the time goes in v1:
time: 92.3 us; the launch traced here: 92.1 us
  Pallas kernels  90.2 us (98%)
  local copies, waits for them, and re-layouts  1.87 us (2%)
    pallas_call x1, Pallas kernels, local(): pl.pallas_call(functools.partial(kernel, sizes), out_shape=jax.ShapeDtype...  90.2 us
    unnamed x1, local copies, waits for them, and re-layouts  1.87 us

profile of v1, /device:TPU:6, one launch (start us, length us, event | category | flops | bytes accessed | tf_op | source)
XLA Modules:
  0.0 92.1 jit_solution(6693088425882128737)
XLA Ops:
  0.0 90.2 %shard_map.100 = bf16[1024,256]{1,0:T(8,128)(2,1)} custom-call(bf16[1024,256]{1,0:T(8,128)(2,1)} %labels_hbm.1, bf16[512,64]{1,0:T(8,128)(2,1)} %bitcast.9, bf16[1024,512]{1,0:T(8,128)(2,1)} %inc_hbm.1, s32[8,128]{1,0:T(8,128)} %bitcast.10, s32[4,128]{1,0:T(4,128)} %bitcast.13, s32[8,128]{1,0:T(8,128)} %bitcast.11, s32[8,128]{1,0:T(8,128)} %bitcast.12, ...), custom_call_target="tpu_custom_call" | custom-call | tf_op jit(solution)/shard_map/pallas_call | solution.py:419
  90.2 1.9 %copy.12 = bf16[1024,256]{1,0:T(8,128)(2,1)} copy(bf16[1024,256]{1,0:T(8,128)(2,1)} %shard_map.100) | data formatting | bytes 1048576

commit v2 on v1

v2 whole, which is shorter than its diff:
```python
import functools

import jax
import jax.numpy as jnp
from jax import lax
from jax.experimental import pallas as pl
from jax.experimental.pallas import tpu as pltpu
from jax.sharding import PartitionSpec as P

ROUNDS = 2
PARTS = 2
LANES = 128
EPS = 1e-05
MESH = pl.DeviceIdType.MESH
F32 = jnp.float32
BF16 = jnp.bfloat16


def iota(shape, dim):
    return lax.broadcasted_iota(jnp.int32, shape, dim)


def dot(a, b):
    return jnp.dot(a, b, preferred_element_type=F32)


def dot_t(a, b):
    return lax.dot_general(a, b, (((1,), (1,)), ((), ())), preferred_element_type=F32)


def tiled(a, count):
    return a if count == 1 else jnp.concatenate([a] * count, axis=1)


def span(first, end, body):
    def step(i, carry):
        body(i)
        return carry

    lax.fori_loop(first, end, step, 0)


def loop(count, body):
    span(0, count, body)


def rows_of(i, count):
    return pl.ds(pl.multiple_of(i * count, count), count)


def kernel(
    sizes,
    labels_hbm,
    tiles_hbm,
    inc_hbm,
    node_hbm,
    edge_hbm,
    mask_hbm,
    seed_hbm,
    block_hbm,
    count_hbm,
    in_hbm,
    out_ref,
    labels,
    tiles,
    inc,
    node_ref,
    edge_ref,
    mask_ref,
    seed_ref,
    block_ref,
    count_ref,
    in_ref,
    inc_t,
    spread,
    spread_t,
    choose,
    choose_t,
    tile_col,
    block_col,
    scale_col,
    seed_col,
    div_col,
    scaled,
    agg,
    edge_sum,
    node_sum,
    fsend,
    frecv,
    bsend,
    brecv,
    in_sem,
    ready,
    fsend_sem,
    frecv_sem,
    bsend_sem,
    brecv_sem,
):
    n, slots, block, width, rows, edges, classes = sizes
    cols = classes // PARTS
    flat = slots * width
    half = flat // 2
    fold = LANES // block
    g, p = lax.axis_index("grp"), lax.axis_index("peer")

    with jax.named_scope("greet"):
        moves = (
            (node_hbm, node_ref),
            (labels_hbm, labels),
            (tiles_hbm, tiles),
            (block_hbm, block_ref),
            (count_hbm, count_ref),
            (in_hbm, in_ref),
            (edge_hbm, edge_ref),
            (mask_hbm, mask_ref),
            (seed_hbm, seed_ref),
            (inc_hbm, inc),
        )
        loads = [pltpu.make_async_copy(src, dst, in_sem.at[k]) for k, (src, dst) in enumerate(moves)]
        for load in loads:
            load.start()

        barrier = pltpu.get_barrier_semaphore()

        def call(j, kind):
            where = (j, p) if kind else (g, j)
            pl.semaphore_signal(barrier, inc=1, device_id=where, device_id_type=MESH)

        def answer(j, kind):
            where = (j, p) if kind else (g, j)
            pl.semaphore_signal(ready.at[n + g if kind else p], inc=1, device_id=where, device_id_type=MESH)

        span(p + 1, n, lambda j: call(j, 0))
        span(g + 1, n, lambda j: call(j, 1))

        @pl.when(p + g > 0)
        def _():
            pl.semaphore_wait(barrier, p + g)

        span(0, p, lambda j: answer(j, 0))
        span(0, g, lambda j: answer(j, 1))

    def column(ref):
        k, lanes = ref.shape
        pick = (iota((k, k * LANES), 1) // LANES == iota((k, k * LANES), 0)).astype(BF16)
        wide = lax.dot_general(ref[...].astype(F32).astype(BF16), pick, (((0,), (0,)), ((), ())), preferred_element_type=F32)
        return [wide[:, i * LANES : (i + 1) * LANES] for i in range(k)]

    with jax.named_scope("scale"):
        loads[0].wait()
        for i, part in enumerate(column(node_ref)):
            scale_col[i * LANES : (i + 1) * LANES, :] = lax.rsqrt(part)
        loads[1].wait()

        for i in range(rows // LANES):
            at = slice(i * LANES, (i + 1) * LANES)
            scaled[at, :] = (labels[at, :].astype(F32) * tiled(scale_col[at, :], classes // LANES)).astype(BF16)

    def pick_rows(first, count, value):
        slot = first + iota((count, slots), 0) // width
        return jnp.where(slot == iota((count, slots), 1), value, 0.0).astype(BF16)

    def slot_col(first, count, ref):
        values = jnp.broadcast_to(ref[...].astype(F32), (LANES, slots)).astype(BF16)
        return dot_t(pick_rows(first, count, 1.0), values)

    def first_product(kind):
        at = slice(kind * half, (kind + 1) * half)
        wide = dot_t(pick_rows(kind * n, half, count_ref[...].astype(F32)), tiles[...])
        same = iota((half, block * width), 0) % width == iota((half, block * width), 1) % width
        gather = (iota((block * width, LANES), 0) // width == iota((block * width, LANES), 1) % block).astype(BF16)
        weight = dot(jnp.where(same, wide, 0.0).astype(BF16), gather)
        place = slot_col(kind * n, half, block_ref)
        tile_col[at, :] = weight
        block_col[at, :] = place
        lane_block = (iota((half, LANES), 1) // block).astype(F32)
        for k in range(rows // LANES):
            piece = jnp.where(place == lane_block + float(k * fold), weight, 0.0)
            spread_t[at, k * LANES : (k + 1) * LANES] = piece.astype(BF16)
        out_product(0, kind)

    def out_product(r, kind):
        at = slice(kind * half, (kind + 1) * half)
        product = dot(spread_t[at, :], scaled[...]).astype(BF16)
        for h in range(PARTS):
            fsend[r, h, at, :] = product[:, h * cols : (h + 1) * cols]

    def copy_to(r, h, kind, other, src, dst, send_sem, recv_sem):
        me = g if kind else p
        pltpu.make_async_remote_copy(
            src_ref=src.at[r, h, rows_of(kind * n + other, width)],
            dst_ref=dst.at[r, h, rows_of(kind * n + me, width)],
            send_sem=send_sem.at[r, h],
            recv_sem=recv_sem.at[r, h, kind],
            device_id=(other, p) if kind else (g, other),
            device_id_type=MESH,
        ).start()

    def around(me, send):
        def wrap(x):
            return jnp.where(x >= n, x - n, x)

        def both(t):
            send(wrap(me + (n // 2) - t))
            send(wrap(me + (n // 2) + t))

        send(wrap(me + n // 2))
        span(1, n // 2, both)

    def keep(r, h, kind, src, dst, send_sem, recv_sem):
        at = rows_of(n + g if kind else p, width)
        pltpu.make_async_copy(src.at[r, h, at], dst.at[r, h, at], recv_sem.at[r, h, kind]).start()

    def send_all(r, h, kind, *way):
        around(g if kind else p, lambda other: copy_to(r, h, kind, other, *way))
        keep(r, h, kind, *way)

    def arrive(r, h, kind, dst, recv_sem):
        part = dst.at[r, h, pl.ds(kind * half, half)]
        pltpu.make_async_copy(part, part, recv_sem.at[r, h, kind]).wait()

    out_way = (fsend, frecv, fsend_sem, frecv_sem)
    back_way = (bsend, brecv, bsend_sem, brecv_sem)

    with jax.named_scope("first_send"):
        for load in loads[2:5]:
            load.wait()
        first_product(0)

        def early(other, h):
            @pl.when(other < p)
            def _():
                copy_to(0, h, 0, other, *out_way)

        def late(other, h):
            if h == 0:
                pl.semaphore_wait(ready.at[other], 1)
            copy_to(0, h, 0, other, *out_way)

        def latest(other, h):
            @pl.when(jnp.logical_and(other > p, other >= n // 2))
            def _():
                late(other, h)

        def across(j, h):
            if h == 0:
                pl.semaphore_wait(ready.at[n + j], 1)
            copy_to(0, h, 1, j, *out_way)

        around(p, lambda other: early(other, 0))
        first_product(1)
        span(0, g, lambda j: copy_to(0, 0, 1, j, *out_way))
        span(g + 1, n, lambda j: across(j, 0))
        for h in range(1, PARTS):
            around(p, lambda other: early(other, h))
        span(p + 1, n // 2, lambda j: late(j, 0))
        around(p, lambda other: latest(other, 0))
        keep(0, 0, 0, *out_way)
        keep(0, 0, 1, *out_way)
        for h in range(1, PARTS):
            span(p + 1, n // 2, lambda j: late(j, h))
            around(p, lambda other: latest(other, h))
            span(0, g, lambda j: copy_to(0, h, 1, j, *out_way))
            span(g + 1, n, lambda j: across(j, h))
            keep(0, h, 0, *out_way)
            keep(0, h, 1, *out_way)

    def build_edge():
        for load in loads[5:7]:
            load.wait()
        loads[9].wait()
        for i, part in enumerate(column(edge_ref)):
            div_col[i * LANES : (i + 1) * LANES, :] = part
        for i in range(rows // LANES):
            at = slice(i * LANES, (i + 1) * LANES)
            inc_t[:, at] = inc[at, :].astype(F32).T.astype(BF16)
        for i in range(flat // LANES):
            at = slice(i * LANES, (i + 1) * LANES)
            row = (iota((LANES, LANES), 0) % width).astype(F32)
            target = slot_col(i * (LANES // width), LANES, in_ref) * float(width) + row
            target_t = target.T
            for k in range(edges // LANES):
                e = slice(k * LANES, (k + 1) * LANES)
                lane = (iota((LANES, LANES), 1) + k * LANES).astype(F32)
                choose_t[at, e] = jnp.where(target == lane, 1.0, 0.0).astype(BF16)
                down = (iota((LANES, LANES), 0) + k * LANES).astype(F32)
                choose[e, at] = jnp.where(target_t == down, 1.0, 0.0).astype(BF16)

    def build_node():
        for load in loads[7:9]:
            load.wait()
        known, class_of = column(mask_ref), column(seed_ref)
        for i in range(rows // LANES):
            seed_col[i * LANES : (i + 1) * LANES, :] = jnp.where(known[i] == 1.0, class_of[i], -1.0)
        for i in range(flat // LANES):
            at = slice(i * LANES, (i + 1) * LANES)
            weight, place = tile_col[at, :].T, block_col[at, :].T
            down_block = (iota((LANES, LANES), 0) // block).astype(F32)
            for k in range(rows // LANES):
                b = slice(k * LANES, (k + 1) * LANES)
                spread[b, at] = jnp.where(place == down_block + float(k * fold), weight, 0.0).astype(BF16)

    near, far = slice(0, half), slice(half, flat)

    for r in range(ROUNDS):
        if r > 0:
            with jax.named_scope("out_send"):
                out_product(r, 0)
                send_all(r, 0, 0, *out_way)
                out_product(r, 1)
                send_all(r, 0, 1, *out_way)
                for h in range(1, PARTS):
                    send_all(r, h, 0, *out_way)
                    send_all(r, h, 1, *out_way)
        else:
            with jax.named_scope("build_edge"):
                build_edge()

        with jax.named_scope("local_edge"):

            def local_edge(i):
                at = rows_of(i, 256)
                edge_sum[at, :] = dot(inc_t[at, :], scaled[...])

            loop(edges // 256, local_edge)

        for h in range(PARTS):
            part = slice(h * cols, (h + 1) * cols)
            with jax.named_scope("edge"):
                arrive(r, h, 1, frecv, frecv_sem)
                edge_sum[:, part] += dot(choose[:, far], frecv[r, h, far, :])
                arrive(r, h, 0, frecv, frecv_sem)
                for i in range(edges // 256):
                    at = slice(i * 256, (i + 1) * 256)
                    total = edge_sum[at, part] + dot(choose[at, near], frecv[r, h, near, :])
                    agg[at, part] = (total / tiled(div_col[at, :], cols // LANES)).astype(BF16)
            with jax.named_scope("back_send"):
                for kind in range(2):
                    at = slice(kind * half, (kind + 1) * half)
                    bsend[r, h, at, :] = dot(choose_t[at, :], agg[:, part]).astype(BF16)
                    send_all(r, h, kind, *back_way)
                if r == 0 and h == PARTS - 1:
                    build_node()
            with jax.named_scope("local_node"):

                def local_node(i):
                    at = rows_of(i, 256)
                    node_sum[at, part] = dot(inc[at, :], agg[:, part])

                loop(rows // 256, local_node)

        for h in range(PARTS):
            part = slice(h * cols, (h + 1) * cols)
            with jax.named_scope("node"):
                arrive(r, h, 1, brecv, brecv_sem)

                def across_node(i):
                    at = rows_of(i, 256)
                    node_sum[at, part] += dot(spread[at, far], brecv[r, h, far, :])

                loop(rows // 256, across_node)
                arrive(r, h, 0, brecv, brecv_sem)
                if h < PARTS - 1:

                    def peer_node(i):
                        at = rows_of(i, 256)
                        node_sum[at, part] += dot(spread[at, near], brecv[r, h, near, :])

                    loop(rows // 256, peer_node)

        with jax.named_scope("finish"):
            for i in range(rows // LANES):
                at = slice(i * LANES, (i + 1) * LANES)
                last = dot(spread[at, near], brecv[r, PARTS - 1, near, :])
                total = node_sum[at, :]
                if PARTS > 1:
                    total = jnp.concatenate([total[:, : classes - cols], total[:, classes - cols :] + last], axis=1)
                else:
                    total = total + last
                mean_square = jnp.sum(total * total, axis=-1, keepdims=True) * (1.0 / classes)
                normed = total * lax.rsqrt(mean_square + EPS)
                known = tiled(seed_col[at, :], classes // LANES)
                seeds = jnp.where(iota((LANES, classes), 1).astype(F32) == known, float(classes) ** 0.5, 0.0)
                current = jnp.where(known >= 0.0, seeds, normed).astype(BF16)
                if r < ROUNDS - 1:
                    scaled[at, :] = (current.astype(F32) * tiled(scale_col[at, :], classes // LANES)).astype(BF16)
                else:
                    out_ref[at, :] = current

    with jax.named_scope("sent"):
        for r in range(ROUNDS):
            for h in range(PARTS):
                for buf, sem in ((fsend, fsend_sem), (bsend, bsend_sem)):
                    sent = buf.at[r, h, pl.ds(0, (slots - 2) * width)]
                    pltpu.make_async_copy(sent, sent, sem.at[r, h]).wait()


def local(labels, node_degree, edge_degree, labeled_mask, seed_labels, local_incidence, tiles, out_block, out_count, in_edge):
    n = lax.axis_size("peer")
    rows, classes = labels.shape
    edges = local_incidence.shape[1]
    _, slots, block, width = tiles.shape
    flat = slots * width
    sizes = (n, slots, block, width, rows, edges, classes)
    travel = (ROUNDS, PARTS, flat, classes // PARTS)
    hbm = pl.BlockSpec(memory_space=pltpu.HBM)
    dma = pltpu.SemaphoreType.DMA
    args = (
        labels,
        tiles[0].transpose(1, 2, 0).reshape(block * width, slots),
        local_incidence,
        node_degree.reshape(rows // LANES, LANES),
        edge_degree.reshape(edges // LANES, LANES),
        labeled_mask.reshape(rows // LANES, LANES),
        seed_labels.reshape(rows // LANES, LANES),
        out_block,
        out_count,
        in_edge,
    )
    return pl.pallas_call(
        functools.partial(kernel, sizes),
        out_shape=pltpu.VMEM((rows, classes), BF16),
        in_specs=[hbm] * len(args),
        out_specs=pl.BlockSpec(memory_space=pltpu.VMEM),
        scratch_shapes=[pltpu.VMEM(a.shape, a.dtype) for a in args]
        + [
            pltpu.VMEM((edges, rows), BF16),
            pltpu.VMEM((rows, flat), BF16),
            pltpu.VMEM((flat, rows), BF16),
            pltpu.VMEM((edges, flat), BF16),
            pltpu.VMEM((flat, edges), BF16),
            pltpu.VMEM((flat, LANES), F32),
            pltpu.VMEM((flat, LANES), F32),
            pltpu.VMEM((rows, LANES), F32),
            pltpu.VMEM((rows, LANES), F32),
            pltpu.VMEM((edges, LANES), F32),
            pltpu.VMEM((rows, classes), BF16),
            pltpu.VMEM((edges, classes), BF16),
            pltpu.VMEM((edges, classes), F32),
            pltpu.VMEM((rows, classes), F32),
            pltpu.VMEM(travel, BF16),
            pltpu.VMEM(travel, BF16),
            pltpu.VMEM(travel, BF16),
            pltpu.VMEM(travel, BF16),
            dma((len(args),)),
            pltpu.SemaphoreType.REGULAR((slots,)),
            dma((ROUNDS, PARTS)),
            dma((ROUNDS, PARTS, 2)),
            dma((ROUNDS, PARTS)),
            dma((ROUNDS, PARTS, 2)),
        ],
        compiler_params=pltpu.CompilerParams(collective_id=0, has_side_effects=True, vmem_limit_bytes=56 << 20),
    )(*args)


def solution(mesh):
    split = ("grp", "peer")
    specs = (
        P(split, None),
        P(split),
        P(split),
        P(split),
        P(split),
        P(split, None),
        P(split, None, None, None),
        P(split, None),
        P(split, None),
        P(split, None),
    )
    return jax.shard_map(local, mesh=mesh, in_specs=specs, out_specs=P(split, None), check_vma=False)
```

time: 92.3 us -> 84.4 us (0.914)
  Pallas kernels: 90.2 us -> 83 us
  local copies, waits for them, and re-layouts: 1.87 us -> 0.8 us
    pallas_call x1, Pallas kernels: 90.2 us -> 83 us  [local(): pl.pallas_call(functools.partial(kernel, sizes), out_shape=pltpu.VMEM((ro...]
    unnamed x1, local copies, waits for them, and re-layouts: 1.87 us -> 0.8 us
where the time goes in v2:
time: 84.4 us; the launch traced here: 83.8 us
  Pallas kernels  83 us (98%)
    pallas_call x1, Pallas kernels, local(): pl.pallas_call(functools.partial(kernel, sizes), out_shape=pltpu.VMEM((ro...  83 us

profile of v2, /device:TPU:6, one launch (start us, length us, event | category | flops | bytes accessed | tf_op | source)
XLA Modules:
  0.0 83.8 jit_solution(9222230673082899314)
XLA Ops:
  0.0 83.0 %shard_map.100 = bf16[1024,256]{1,0:T(8,128)(2,1)S(1)} custom-call(bf16[1024,256]{1,0:T(8,128)(2,1)} %labels_hbm.1, bf16[512,64]{1,0:T(8,128)(2,1)} %bitcast.9, bf16[1024,512]{1,0:T(8,128)(2,1)} %inc_hbm.1, s32[8,128]{1,0:T(8,128)} %bitcast.10, s32[4,128]{1,0:T(4,128)} %bitcast.13, s32[8,128]{1,0:T(8,128)} %bitcast.11, s32[8,128]{1,0:T(8,128)} %bitcast.12, ...), custom_call_target="tpu_custom_call" | custom-call | tf_op jit(solution)/shard_map/pallas_call | solution.py:420
  83.0 0.8 copy.12
